TPU v7x, 32 devices: a whole 2x2x4 slice. The times are simulated.
32 devices in a mesh: expert: 8 (over z, y), tensor: 4 (over x, core).
Axes of the slice: x: 2, y: 2, z: 4, core: 2. Of those that a mesh axis runs over, the one named last changes fastest.
Arguments:
- tokens: bfloat16 [4096, 2048], P('expert'), may hold values from -15 to 15
- gain_attn: float32 [2048], replicated, may hold values from 0.5 to 1.5
- w_query: bfloat16 [2048, 2048], P(None, 'tensor'), may hold values from -0.125 to 0.125
- w_key: bfloat16 [2048, 2048], P(None, 'tensor'), may hold values from -0.125 to 0.125
- w_value: bfloat16 [2048, 2048], P(None, 'tensor'), may hold values from -0.125 to 0.125
- w_out: bfloat16 [2048, 2048], P('tensor'), may hold values from -2 to 2
- gain_moe: float32 [2048], replicated, may hold values from 0.5 to 1.5
- w_router: bfloat16 [2048, 64], replicated, may hold values from -0.0625 to 0.0625
- w_gate: bfloat16 [64, 2048, 1024], P('expert', None, 'tensor'), may hold values from -0.125 to 0.125
- w_up: bfloat16 [64, 2048, 1024], P('expert', None, 'tensor'), may hold values from -0.125 to 0.125
- w_down: bfloat16 [64, 1024, 2048], P('expert', 'tensor'), may hold values from -0.75 to 0.75
- expert_ids: int32 [4096, 8], P(('expert', 'tensor')), may hold values from 0 to 63, all different within a row; in each aligned block of 128 rows (0 to 127, 128 to 255, ...) at most 24 rows name the same one
- cotangent: bfloat16 [4096, 2048], P(('expert', 'tensor')), may hold values from -6 to 6
Outputs:
- mixed: bfloat16 [4096, 2048], P(('expert', 'tensor'))
- grad_tokens: float32 [4096, 2048], P(('expert', 'tensor'))
- grad_gain_attn: float32 [2048], replicated
- grad_w_query: float32 [2048, 2048], P(None, 'tensor')
- grad_w_key: float32 [2048, 2048], P(None, 'tensor')
- grad_w_value: float32 [2048, 2048], P(None, 'tensor')
- grad_w_out: float32 [2048, 2048], P('tensor')
- grad_gain_moe: float32 [2048], replicated
- grad_w_router: float32 [2048, 64], replicated
- grad_w_gate: float32 [64, 2048, 1024], P('expert', None, 'tensor')
- grad_w_up: float32 [64, 2048, 1024], P('expert', None, 'tensor')
- grad_w_down: float32 [64, 1024, 2048], P('expert', 'tensor')
Inputs may be any that keep to these rules, and one draw needn't show every extreme that they name: `expert_ids`: each row names 8 different experts; among the rows of one device (aligned blocks of 128 rows) no expert is named more than 24 times, and in some blocks one is named exactly 24 times.
All inputs are finite; a program needn't handle non-finite values.
Results may differ from a plain program's by a relative error of at most 0.018.
Values may be sent and summed in bfloat16 or wider, within the bound.
No kernel may reach another device: no remote copies, remote signals or barrier semaphores. Data moves between devices by JAX's collectives and lax.ppermute only.
A program may use at most 448 MiB of HBM per device.

v0:
```python
import jax
import jax.numpy as jnp
from jax import lax
from jax.sharding import PartitionSpec as P

HD = 128


eps = 1e-06
theta_base = 10000.0
masked = -1e30


def rope_tables(seq_length, head_size):
    half_dim = head_size // 2
    frequency = jnp.exp(
        -jnp.log(theta_base) * jnp.arange(half_dim, dtype=jnp.float32) * (2.0 / head_size)
    )
    angles = jnp.arange(seq_length, dtype=jnp.float32)[:, None] * frequency[None, :]
    return (jnp.cos(angles)[:, None, :], jnp.sin(angles)[:, None, :])


def rotate(source, cosine_table, sine_table):
    half_dim = source.shape[-1] // 2
    first_half = source[..., :half_dim]
    second = source[..., half_dim:]
    return jnp.concatenate(
        [
            first_half * cosine_table - second * sine_table,
            second * cosine_table + first_half * sine_table,
        ],
        axis=-1,
    )


def norm_forward(source, gain_vec):
    inverse = lax.rsqrt(jnp.mean(source * source, axis=-1, keepdims=True) + eps)
    return (inverse, source * inverse * gain_vec)


def norm_backward(source, inverse, gain_vec, grad_in):
    scaled = gain_vec * grad_in
    grad_source = inverse * scaled - source * inverse**3 * jnp.mean(
        scaled * source, axis=-1, keepdims=True
    )
    grad_gain = jnp.sum(grad_in * source * inverse, axis=0)
    return (grad_source, grad_gain)


def block_scores(q_block, key_rows, first_row, score_scale):
    scores = (
        jnp.einsum("qgrd,kgd->grqk", q_block, key_rows, preferred_element_type=jnp.float32)
        * score_scale
    )
    row_ids = first_row + jnp.arange(q_block.shape[0], dtype=jnp.int32)
    allowed = row_ids[:, None] >= jnp.arange(key_rows.shape[0], dtype=jnp.int32)[None, :]
    return jnp.where(allowed, scores, masked)


def on_device(
    tokens,
    gain_attn,
    w_query,
    w_key,
    w_value,
    w_out,
    gain_moe,
    w_router,
    w_gate,
    w_up,
    w_down,
    expert_ids,
    cotangent,
):
    seq_length, model_width = tokens.shape
    block_len, top_count = expert_ids.shape
    expert_count = w_router.shape[1]
    local_experts = w_gate.shape[0]
    local_heads = w_query.shape[1] // HD
    local_groups = w_key.shape[1] // HD
    group_size = local_heads // local_groups
    owners = lax.axis_size("expert")
    quarter = lax.axis_index("tensor")
    capacity = 3 * block_len * top_count // (2 * expert_count)
    block_rows = min(512, seq_length)
    block_count = seq_length // block_rows
    score_scale = HD ** (-0.5)
    first_own = quarter * block_len
    inputs = tokens.astype(jnp.float32)
    inverse_one, normed_one = norm_forward(inputs, gain_attn)
    hidden_one = normed_one.astype(jnp.bfloat16)
    cosine_table, sine_table = rope_tables(seq_length, HD)

    def rope_heads(source):
        return rotate(source, cosine_table, sine_table)

    query_raw = jnp.dot(hidden_one, w_query, preferred_element_type=jnp.float32).reshape(
        seq_length, local_heads, HD
    )
    key_raw = jnp.dot(hidden_one, w_key, preferred_element_type=jnp.float32).reshape(
        seq_length, local_groups, HD
    )
    queries = rope_heads(query_raw).astype(jnp.bfloat16)
    key_rows = rope_heads(key_raw).astype(jnp.bfloat16)
    value_rows = (
        jnp.dot(hidden_one, w_value, preferred_element_type=jnp.float32)
        .astype(jnp.bfloat16)
        .reshape(seq_length, local_groups, HD)
    )
    query_blocks = queries.reshape(block_count, block_rows, local_groups, group_size, HD)
    starts = jnp.arange(block_count, dtype=jnp.int32) * block_rows

    def attend_block(packed):
        first_row, q_block = packed
        scores = block_scores(q_block, key_rows, first_row, score_scale)
        row_max = jnp.max(scores, axis=-1, keepdims=True)
        exponent = jnp.exp(scores - row_max)
        row_total = jnp.sum(exponent, axis=-1, keepdims=True)
        weights = (exponent / row_total).astype(jnp.bfloat16)
        head_out = jnp.einsum(
            "grqk,kgd->qgrd", weights, value_rows, preferred_element_type=jnp.float32
        )
        return (head_out.astype(jnp.bfloat16), (row_max + jnp.log(row_total))[..., 0])

    head_blocks, log_totals = lax.map(attend_block, (starts, query_blocks))
    head_rows = head_blocks.reshape(seq_length, local_heads * HD)
    attention = lax.psum_scatter(
        jnp.dot(head_rows, w_out, preferred_element_type=jnp.float32),
        "tensor",
        scatter_dimension=0,
        tiled=True,
    )
    own_inputs = lax.dynamic_slice_in_dim(inputs, first_own, block_len, 0)
    own_inverse = lax.dynamic_slice_in_dim(inverse_one, first_own, block_len, 0)
    middle = own_inputs + attention
    inverse_two, normed_two = norm_forward(middle, gain_moe)
    hidden_two = normed_two.astype(jnp.bfloat16)
    logits = jnp.dot(hidden_two, w_router, preferred_element_type=jnp.float32)
    expert_range = jnp.arange(expert_count, dtype=jnp.int32)
    matches = expert_ids[:, :, None] == expert_range[None, None, :]
    chosen = jnp.sum(jnp.where(matches, logits[:, None, :], 0.0), axis=2)
    gate_weights = jax.nn.softmax(chosen, axis=-1)
    expert_hits = jnp.sum(matches.astype(jnp.int32), axis=1)
    earlier = jnp.cumsum(expert_hits, axis=0) - expert_hits
    slot_of = jnp.sum(jnp.where(matches, earlier[:, None, :], 0), axis=2)
    place = (slot_of * expert_count + expert_ids).reshape(-1)
    token_rows = jnp.broadcast_to(
        hidden_two[:, None, :], (block_len, top_count, model_width)
    ).reshape(block_len * top_count, model_width)
    grad_out = cotangent.astype(jnp.float32)
    gated_grads = (
        (gate_weights[:, :, None] * grad_out[:, None, :])
        .astype(jnp.bfloat16)
        .reshape(block_len * top_count, model_width)
    )
    empty = jnp.zeros((capacity * expert_count, model_width), jnp.bfloat16)
    send_rows = empty.at[place].set(token_rows).reshape(capacity, expert_count, model_width)
    send_grads = empty.at[place].set(gated_grads).reshape(capacity, expert_count, model_width)
    arrived_rows, arrived_grads = (
        lax.all_to_all(send_rows, "expert", split_axis=1, concat_axis=1, tiled=True),
        lax.all_to_all(send_grads, "expert", split_axis=1, concat_axis=1, tiled=True),
    )
    routed = arrived_rows.reshape(capacity, owners, local_experts, model_width)
    grads_in = arrived_grads.reshape(capacity, owners, local_experts, model_width)
    all_rows, all_grads = (
        lax.all_gather(routed, "tensor", axis=0, tiled=True),
        lax.all_gather(grads_in, "tensor", axis=0, tiled=True),
    )
    gate_pre = jnp.einsum("csld,ldf->cslf", all_rows, w_gate, preferred_element_type=jnp.float32)
    up_pre = jnp.einsum("csld,ldf->cslf", all_rows, w_up, preferred_element_type=jnp.float32)
    sigmoid_gate = jax.nn.sigmoid(gate_pre)
    silu_gate = gate_pre * sigmoid_gate
    activation = (silu_gate * up_pre).astype(jnp.bfloat16)
    grad_w_down = jnp.einsum(
        "cslf,csld->lfd", activation, all_grads, preferred_element_type=jnp.float32
    )
    grad_act = jnp.einsum("csld,lfd->cslf", all_grads, w_down, preferred_element_type=jnp.float32)
    grad_gate = (grad_act * up_pre * sigmoid_gate * (1.0 + gate_pre * (1.0 - sigmoid_gate))).astype(
        jnp.bfloat16
    )
    grad_up = (grad_act * silu_gate).astype(jnp.bfloat16)
    grad_w_gate = jnp.einsum(
        "csld,cslf->ldf", all_rows, grad_gate, preferred_element_type=jnp.float32
    )
    grad_w_up = jnp.einsum("csld,cslf->ldf", all_rows, grad_up, preferred_element_type=jnp.float32)
    forward_term = jnp.einsum(
        "cslf,lfd->csld", activation, w_down, preferred_element_type=jnp.float32
    )
    back_term = jnp.einsum("cslf,ldf->csld", grad_gate, w_gate, preferred_element_type=jnp.float32)
    back_term = back_term + jnp.einsum(
        "cslf,ldf->csld", grad_up, w_up, preferred_element_type=jnp.float32
    )
    both_terms = lax.psum_scatter(
        jnp.concatenate([forward_term, back_term], axis=3).astype(jnp.bfloat16),
        "tensor",
        scatter_dimension=0,
        tiled=True,
    )
    returned = both_terms[..., :model_width]
    row_grads = both_terms[..., model_width:]
    returned_home, row_grads_home = (
        lax.all_to_all(
            returned.reshape(capacity, expert_count, model_width),
            "expert",
            split_axis=1,
            concat_axis=1,
            tiled=True,
        ),
        lax.all_to_all(
            row_grads.reshape(capacity, expert_count, model_width),
            "expert",
            split_axis=1,
            concat_axis=1,
            tiled=True,
        ),
    )
    picked = returned_home.reshape(capacity * expert_count, model_width)[place].reshape(
        block_len, top_count, model_width
    )
    mixture = jnp.sum(gate_weights[:, :, None] * picked, axis=1)
    mixed_out = (middle + mixture).astype(jnp.bfloat16)
    grad_gates = jnp.sum(picked * grad_out[:, None, :], axis=2)
    grad_picked = row_grads_home.reshape(capacity * expert_count, model_width)[place].reshape(
        block_len, top_count, model_width
    )
    grad_hidden_disp = jnp.einsum(
        "lk,lkd->ld",
        jnp.ones((block_len, top_count), jnp.bfloat16),
        grad_picked,
        preferred_element_type=jnp.float32,
    )
    grad_chosen = gate_weights * (
        grad_gates - jnp.sum(gate_weights * grad_gates, axis=-1, keepdims=True)
    )
    grad_logits = jnp.sum(jnp.where(matches, grad_chosen[:, :, None], 0.0), axis=1).astype(
        jnp.bfloat16
    )
    grad_router = jnp.einsum(
        "ld,le->de", hidden_two, grad_logits, preferred_element_type=jnp.float32
    )
    grad_hidden_two = grad_hidden_disp + jnp.einsum(
        "le,de->ld", grad_logits, w_router, preferred_element_type=jnp.float32
    )
    grad_normed_two, grad_gain_moe = norm_backward(middle, inverse_two, gain_moe, grad_hidden_two)
    grad_middle = grad_out + grad_normed_two
    grad_attn = grad_middle.astype(jnp.bfloat16)
    grad_attn_all = lax.all_gather(grad_attn, "tensor", axis=0, tiled=True)
    grad_w_out = jnp.einsum(
        "lh,ld->hd", head_rows, grad_attn_all, preferred_element_type=jnp.float32
    )
    grad_heads = jnp.einsum(
        "ld,hd->lh", grad_attn_all, w_out, preferred_element_type=jnp.float32
    ).astype(jnp.bfloat16)
    grad_blocks = grad_heads.reshape(block_count, block_rows, local_groups, group_size, HD)

    def back_block(carried, packed):
        grad_keys, grad_values = carried
        first_row, q_block, g_block, lse_block = packed
        scores = block_scores(q_block, key_rows, first_row, score_scale)
        probability = jnp.exp(scores - lse_block[..., None])
        grad_values = grad_values + jnp.einsum(
            "grqk,qgrd->kgd",
            probability.astype(jnp.bfloat16),
            g_block,
            preferred_element_type=jnp.float32,
        )
        grad_prob = jnp.einsum(
            "qgrd,kgd->grqk", g_block, value_rows, preferred_element_type=jnp.float32
        )
        row_delta = jnp.sum(probability * grad_prob, axis=-1, keepdims=True)
        grad_scores = (probability * (grad_prob - row_delta)).astype(jnp.bfloat16)
        grad_query = (
            jnp.einsum("grqk,kgd->qgrd", grad_scores, key_rows, preferred_element_type=jnp.float32)
            * score_scale
        )
        grad_keys = (
            grad_keys
            + jnp.einsum("grqk,qgrd->kgd", grad_scores, q_block, preferred_element_type=jnp.float32)
            * score_scale
        )
        return ((grad_keys, grad_values), grad_query)

    zero_keys = jnp.zeros((seq_length, local_groups, HD), jnp.float32)
    (grad_keys, grad_values), grad_query_blocks = lax.scan(
        back_block, (zero_keys, zero_keys), (starts, query_blocks, grad_blocks, log_totals)
    )
    grad_query = grad_query_blocks.reshape(seq_length, local_heads, HD)
    grad_query_raw = (
        jax.vjp(rope_heads, query_raw)[1](grad_query)[0]
        .reshape(seq_length, local_heads * HD)
        .astype(jnp.bfloat16)
    )
    grad_key_raw = (
        jax.vjp(rope_heads, key_raw)[1](grad_keys)[0]
        .reshape(seq_length, local_groups * HD)
        .astype(jnp.bfloat16)
    )
    grad_value_raw = grad_values.reshape(seq_length, local_groups * HD).astype(jnp.bfloat16)
    grad_w_query = jnp.einsum(
        "ld,lh->dh", hidden_one, grad_query_raw, preferred_element_type=jnp.float32
    )
    grad_w_key = jnp.einsum(
        "ld,lh->dh", hidden_one, grad_key_raw, preferred_element_type=jnp.float32
    )
    grad_w_value = jnp.einsum(
        "ld,lh->dh", hidden_one, grad_value_raw, preferred_element_type=jnp.float32
    )
    term = jnp.einsum("lh,dh->ld", grad_query_raw, w_query, preferred_element_type=jnp.float32)
    term = term + jnp.einsum("lh,dh->ld", grad_key_raw, w_key, preferred_element_type=jnp.float32)
    grad_hidden_one = lax.psum_scatter(
        (
            term
            + jnp.einsum("lh,dh->ld", grad_value_raw, w_value, preferred_element_type=jnp.float32)
        ).astype(jnp.bfloat16),
        "tensor",
        scatter_dimension=0,
        tiled=True,
    ).astype(jnp.float32)
    grad_normed_one, grad_gain_attn = norm_backward(
        own_inputs, own_inverse, gain_attn, grad_hidden_one
    )
    grad_tokens = grad_middle + grad_normed_one
    attn_sums = lax.psum((grad_w_query, grad_w_key, grad_w_value, grad_w_out), "expert")
    small_sums = lax.psum((grad_gain_attn, grad_gain_moe, grad_router), ("expert", "tensor"))
    return (
        mixed_out,
        grad_tokens,
        small_sums[0],
        attn_sums[0],
        attn_sums[1],
        attn_sums[2],
        attn_sums[3],
        small_sums[1],
        small_sums[2],
        grad_w_gate,
        grad_w_up,
        grad_w_down,
    )


def solution(mesh):
    return jax.shard_map(
        on_device,
        mesh=mesh,
        in_specs=(
            P("expert", None),
            P(),
            P(None, "tensor"),
            P(None, "tensor"),
            P(None, "tensor"),
            P("tensor", None),
            P(),
            P(),
            P("expert", None, "tensor"),
            P("expert", None, "tensor"),
            P("expert", "tensor", None),
            P(("expert", "tensor"), None),
            P(("expert", "tensor"), None),
        ),
        out_specs=(
            P(("expert", "tensor"), None),
            P(("expert", "tensor"), None),
            P(),
            P(None, "tensor"),
            P(None, "tensor"),
            P(None, "tensor"),
            P("tensor", None),
            P(),
            P(),
            P("expert", None, "tensor"),
            P("expert", None, "tensor"),
            P("expert", "tensor", None),
        ),
        check_vma=False,
    )
```

profile of v0, /device:TPU:0, one launch (start us, length us, event | category | flops | bytes accessed | tf_op | source)
XLA Modules:
  0.0 2235.5 jit_solution(4899526495034799679)
XLA Ops:
  47.3 42.3 %reduce-scatter.7.cloned.1.call-done = f32[128,2048]{1,0:T(8,128)} async-done(((f32[512,2048]{1,0:T(8,128)}), f32[128,2048]{1,0:T(8,128)}) %reduce-scatter.7.cloned.1.call-update) | async-done | bytes 1048592 | tf_op jit(solution)/shard_map/reduce_scatter | solution.py:127
  108.9 143.8 %all_to_all.20 = bf16[24,64,2048]{2,0,1:T(8,128)(2,1)S(1)} all-to-all(bf16[24,64,2048]{2,0,1:T(8,128)(2,1)S(1)} %copy.180), channel_id=1, replica_groups=mesh['expert'=8,'tensor'=4] {'expert'}, dimensions={1} | all-to-all | bytes 12582912 | tf_op jit(solution)/shard_map/all_to_all | solution.py:160
  283.5 140.9 %all_to_all.21 = bf16[24,64,2048]{2,0,1:T(8,128)(2,1)S(1)} all-to-all(bf16[24,64,2048]{2,0,1:T(8,128)(2,1)S(1)} %copy.184), channel_id=1, replica_groups=mesh['expert'=8,'tensor'=4] {'expert'}, dimensions={1} | all-to-all | bytes 12582912 | tf_op jit(solution)/shard_map/all_to_all | solution.py:161
  431.0 21.3 fusion.8
  452.3 130.9 %all-gather.6.cloned.1.call-done = bf16[96,8,8,2048]{3,1,0,2:T(8,128)(2,1)} async-done(((bf16[24,8,8,2048]{3,1,0,2:T(8,128)(2,1)}), bf16[96,8,8,2048]{3,1,0,2:T(8,128)(2,1)}) %all-gather.6.cloned.1.call-update) | async-done | bytes 25165840 | tf_op jit(solution)/shard_map/all_gather | solution.py:167
  583.1 16.8 fusion.10
  599.9 21.6 fusion.18
  621.5 15.1 convert_bitcast_fusion
  636.7 22.4 %fusion.6 = f32[8,96,8,2048]{3,2,1,0:T(8,128)} fusion(bf16[96,8,8,256]{3,1,0,2:T(8,128)(2,1)} %get-tuple-element.78, bf16[8,2048,256]{2,1,0:T(8,128)(2,1)} %param.21), kind=kOutput, calls=%fused_computation.15 | convolution fusion | flops 6442450944 | bytes 61865984 | tf_op jit(solution)/shard_map/cslf,ldf->csld/dot_general | solution.py:189
  659.0 30.0 %fusion = bf16[96,8,8,2048]{3,1,0,2:T(8,128)(2,1)} fusion(f32[8,96,8,2048]{3,2,1,0:T(8,128)} %fusion.6, bf16[96,8,8,256]{3,1,0,2:T(8,128)(2,1)} %get-tuple-element.79, bf16[8,2048,256]{2,1,0:T(8,128)(2,1)} %param.22), kind=kOutput, calls=%fused_computation.6 | convolution fusion | flops 6467616768 | bytes 87031808 | tf_op jit(solution)/shard_map/cslf,ldf->csld/dot_general | solution.py:190
  689.1 33.9 %pad_maximum_fusion = bf16[96,8,8,4096]{3,1,0,2:T(8,128)(2,1)} fusion(bf16[96,8,8,2048]{3,1,0,2:T(8,128)(2,1)} %fusion, bf16[96,8,8,2048]{3,1,0,2:T(8,128)(2,1)} %convert_bitcast_fusion), kind=kLoop, calls=%fused_computation.4 | loop fusion | flops 100663296 | bytes 100663296 | tf_op jit(solution)/shard_map/concatenate | solution.py:194
  723.0 33.8 %copy.228 = bf16[96,8,8,4096]{3,1,2,0:T(8,128)(2,1)} copy(bf16[96,8,8,4096]{3,1,0,2:T(8,128)(2,1)} %pad_maximum_fusion) | data formatting | bytes 100663296
  756.8 42.8 %copy.237 = bf16[12,8,64,4096]{3,1,2,0:T(8,128)(2,1)} copy(bf16[12,8,64,4096]{3,2,1,0:T(8,128)(2,1)} %bitcast.218) | data formatting | bytes 100663296
  799.6 343.3 %reduce-scatter.11.cloned.1.call-done = bf16[24,262144]{1,0:T(8,128)(2,1)} async-done(((bf16[96,262144]{1,0:T(8,128)(2,1)}), bf16[24,262144]{1,0:T(8,128)(2,1)}) %reduce-scatter.11.cloned.1.call-update) | async-done | bytes 12582928
  1188.4 124.9 %all-to-all-done.3 = bf16[24,64,2048]{2,0,1:T(8,128)(2,1)} async-done(((bf16[24,64,2048]{2,0,1:T(8,128)(2,1)}), bf16[24,64,2048]{2,0,1:T(8,128)(2,1)}, u32[]{:S(2)}, u32[]{:S(2)}) %all-to-all-start.3) | async-done | bytes 6291488 | tf_op jit(solution)/shard_map/all_to_all | solution.py:209
  1329.1 12.8 gather_fusion.1
  1346.3 109.2 %all-to-all-done.2 = bf16[24,64,2048]{2,0,1:T(8,128)(2,1)} async-done(((bf16[24,64,2048]{2,0,1:T(8,128)(2,1)}), bf16[24,64,2048]{2,0,1:T(8,128)(2,1)}, u32[]{:S(2)}, u32[]{:S(2)}) %all-to-all-start.2) | async-done | bytes 6291488 | tf_op jit(solution)/shard_map/all_to_all | solution.py:202
  1464.3 12.4 gather_fusion
  1490.0 19.4 convolution_bitcast_fusion
  1530.8 20.5 convolution_bitcast_fusion.2
  1566.3 20.0 convolution_bitcast_fusion.1
  1588.0 39.4 %all-reduce.4 = (f32[2048]{0:T(1024)}, f32[2048]{0:T(1024)}) all-reduce(f32[2048]{0:T(1024)S(1)} %get-tuple-element.48, f32[2048]{0:T(1024)S(1)} %copy-done.65), channel_id=1, replica_groups=mesh['expert'=8,'tensor'=4] {'expert','tensor'}, use_global_device_ids=true, to_apply=%region_23.24 | all-reduce | flops 4096 | bytes 32768 | tf_op jit(solution)/shard_map/psum | solution.py:324
  1630.2 66.1 %all-reduce.9.cloned.1.call-done = f32[2048,64]{0,1:T(8,128)} async-done(((f32[2048,64]{0,1:T(8,128)}), f32[2048,64]{0,1:T(8,128)}) %all-reduce.9.cloned.1.call-update) | async-done | bytes 524304 | tf_op jit(solution)/shard_map/psum | solution.py:324
  1696.3 517.0 %all-reduce.11.cloned.1.call-done = (f32[2048,512]{1,0:T(8,128)}, f32[2048,512]{1,0:T(8,128)}, f32[2048,512]{1,0:T(8,128)}, f32[512,2048]{1,0:T(8,128)}) async-done(((f32[2048,512]{1,0:T(8,128)}, f32[2048,512]{1,0:T(8,128)}, f32[2048,512]{1,0:T(8,128)}, f32[512,2048]{1,0:T(8,128)}), (f32[2048,512]{1,0:T(8,128)}, f32[2048,512]{1,0:T(8,128)}, f32[2048,512]{1,0:T(8,128)}, ...) | async-done | bytes 16777232 | tf_op jit(solution)/shard_map/psum | solution.py:323
  (260 shorter events, 239.4 us)
Async XLA Ops:
  7.2 31.7 %copy-start = (bf16[512,2048]{1,0:T(8,128)(2,1)S(1)}, bf16[512,2048]{1,0:T(8,128)(2,1)}, u32[]{:S(2)}) copy-start(bf16[512,2048]{1,0:T(8,128)(2,1)} %param.18) | copy-start | bytes 6291460
  7.2 82.3 %reduce-scatter.7.cloned.1.call-start = ((), (), s32[]{:S(2)}) async-start(), calls=%async_computation.7 | async-start | bytes 5242880 | tf_op jit(solution)/shard_map/reduce_scatter | solution.py:127
  42.2 388.8 %all-gather.4.cloned.1.call-start = ((), (), s32[]{:S(2)}) async-start(), calls=%async_computation.8 | async-start | bytes 31457280 | tf_op jit(solution)/shard_map/all_gather | solution.py:166
  42.4 49.8 %copy-start.59 = (f32[2048]{0:T(1024)S(1)}, f32[2048]{0:T(1024)}, u32[]{:S(2)}) copy-start(f32[2048]{0:T(1024)} %param.19) | copy-start | bytes 24580
  47.3 216.3 %copy-start.66 = (s32[1024,1]{0,1:T(1,128)}, s32[1024,1]{0,1:T(1,128)S(1)}, u32[]{:S(2)}) copy-start(s32[1024,1]{0,1:T(1,128)S(1)} %compare_select_fusion) | copy-start | bytes 12292
  259.1 324.0 %all-gather.6.cloned.1.call-start = ((), (), s32[]{:S(2)}) async-start(), calls=%async_computation.9 | async-start | bytes 31457280 | tf_op jit(solution)/shard_map/all_gather | solution.py:167
  260.3 23.1 %copy-start.8 = (f32[128,2048]{1,0:T(8,128)}, f32[128,2048]{1,0:T(8,128)S(1)}, u32[]{:S(2)}) copy-start(f32[128,2048]{1,0:T(8,128)S(1)} %convert_element_type.119) | copy-start | bytes 3145732
  430.7 712.2 %reduce-scatter.11.cloned.1.call-start = ((), (), s32[]{:S(2)}) async-start(), calls=%async_computation.13 | async-start | bytes 62914560
  1169.4 143.9 %all-to-all-start.3 = ((bf16[24,64,2048]{2,0,1:T(8,128)(2,1)}), bf16[24,64,2048]{2,0,1:T(8,128)(2,1)}, u32[]{:S(2)}, u32[]{:S(2)}) async-start(bf16[24,64,2048]{2,0,1:T(8,128)(2,1)} %copy.191), calls=%async_computation.4 | async-start | bytes 12582912 | tf_op jit(solution)/shard_map/all_to_all | solution.py:209
  1188.4 131.0 %copy-start.67 = (s32[1024,1]{0,1:T(1,128)S(1)}, s32[1024,1]{0,1:T(1,128)}, u32[]{:S(2)}) copy-start(s32[1024,1]{0,1:T(1,128)} %copy-done.66) | copy-start | bytes 12292
  1188.4 131.1 %copy-start.62 = (f32[4,512]{1,0:T(4,128)S(1)}, f32[4,512]{1,0:T(4,128)}, u32[]{:S(2)}) copy-start(f32[4,512]{1,0:T(4,128)} %copy-done.61) | copy-start | bytes 24580
  1188.4 131.1 %copy-start.64 = (f32[4,512]{1,0:T(4,128)S(1)}, f32[4,512]{1,0:T(4,128)}, u32[]{:S(2)}) copy-start(f32[4,512]{1,0:T(4,128)} %copy-done.63) | copy-start | bytes 24580
  1313.4 142.1 %all-to-all-start.2 = ((bf16[24,64,2048]{2,0,1:T(8,128)(2,1)}), bf16[24,64,2048]{2,0,1:T(8,128)(2,1)}, u32[]{:S(2)}, u32[]{:S(2)}) async-start(bf16[24,64,2048]{2,0,1:T(8,128)(2,1)} %copy.188), calls=%async_computation.3 | async-start | bytes 12582912 | tf_op jit(solution)/shard_map/all_to_all | solution.py:202
  1318.1 192.7 %all-gather.8.cloned.1.call-start = ((), (), s32[]{:S(2)}) async-start(), calls=%async_computation.10 | async-start | bytes 2621440 | tf_op jit(solution)/shard_map/all_gather | solution.py:247
  1489.9 96.4 %reduce-scatter.9.cloned.1.call-start = ((), (), s32[]{:S(2)}) async-start(), calls=%async_computation.11 | async-start | bytes 2621440 | tf_op jit(solution)/shard_map/reduce_scatter | solution.py:310
  1530.7 165.6 %all-reduce.9.cloned.1.call-start = ((), (), s32[]{:S(2)}) async-start(), calls=%async_computation.12 | async-start | bytes 1048576 | tf_op jit(solution)/shard_map/psum | solution.py:324
  1530.7 21.7 copy-start.5
  1530.8 21.7 copy-start.14
  1530.8 21.7 copy-start.43
  1530.8 21.7 copy-start.56
  1552.4 660.9 %all-reduce.11.cloned.1.call-start = ((), (), s32[]{:S(2)}) async-start(), calls=%async_computation.14 | async-start | bytes 33554432 | tf_op jit(solution)/shard_map/psum | solution.py:323
  1566.3 21.7 copy-start.65
  1566.3 61.2 %copy-start.25 = (f32[128,2048]{1,0:T(8,128)S(1)}, f32[128,2048]{1,0:T(8,128)}, u32[]{:S(2)}) copy-start(f32[128,2048]{1,0:T(8,128)} %get-tuple-element.72) | copy-start | bytes 3145732
  1566.3 61.2 %copy-start.72 = (f32[128]{0:T(128)S(1)}, f32[128]{0:T(128)}, u32[]{:S(2)}) copy-start(f32[128]{0:T(128)} %get-tuple-element.69) | copy-start | bytes 1540
  (59 other events, 339.9 us)
Sparse Core Ops, SparseCore 0:
  42.3 47.2 reduce-scatter.6
  259.2 152.5 all-gather.3
  430.8 152.2 all-gather.5
  799.7 343.1 reduce-scatter.10
  1490.1 20.7 all-gather.7
  1530.8 31.4 reduce-scatter.8
  1568.4 127.8 all-reduce.8
  1701.7 511.5 all-reduce.10
where the time goes:
time: 2240 us
  waiting for transfers between devices  1340 us (60%)
  blocking collectives  324 us (14%)
  matrix products  240 us (11%)
  local copies, waits for them, and re-layouts  228 us (10%)
  other arithmetic  81.8 us (4%)
    psum x1, waiting for transfers between devices, on_device(): lax.psum((grad_w_query, grad_w_key, grad_w_value, grad_w_out), 'expert')  517 us
    unnamed x9, waiting for transfers between devices  343 us
    all_to_all x1, blocking collectives, on_device(): lax.all_to_all(send_rows, 'expert', split_axis=1, concat_axis=1, tiled=True)  144 us
    all_to_all x1, blocking collectives, on_device(): lax.all_to_all(send_grads, 'expert', split_axis=1, concat_axis=1, tiled=T...  141 us
    all_gather x1, waiting for transfers between devices, on_device(): lax.all_gather(grads_in, 'tensor', axis=0, tiled=True)  131 us
    unnamed x160, local copies, waits for them, and re-layouts  127 us
    all_to_all x1, waiting for transfers between devices, on_device(): lax.all_to_all(row_grads.reshape(capacity, expert_count, model_width), 'e...  125 us
    all_to_all x1, waiting for transfers between devices, on_device(): lax.all_to_all(returned.reshape(capacity, expert_count, model_width), 'ex...  109 us
  transfers between devices with their start and end apart: 10, of which 8 were waited for; matrix products, arithmetic and copies ran while one was open for 8% of the time, Pallas kernels for 0%

commit v1 on v0

--- a/solution.py
+++ b/solution.py
@@ -9,6 +9,10 @@
 eps = 1e-06
 theta_base = 10000.0
 masked = -1e30
+
+BOTH = ("expert", "tensor")
+CORE, ACROSS, ASIDE = 1, 2, 4
+PLANES = (0, 8, 16, 24)
 
 
 def rope_tables(seq_length, head_size):
@@ -57,7 +61,7 @@
     return jnp.where(allowed, scores, masked)
 
 
-def on_device(
+def routed_layer(
     tokens,
     gain_attn,
     w_query,
@@ -336,6 +340,332 @@
         grad_w_up,
         grad_w_down,
     )
+
+
+def gathered_layer(
+    tokens,
+    gain_attn,
+    w_query,
+    w_key,
+    w_value,
+    w_out,
+    gain_moe,
+    w_router,
+    w_gate,
+    w_up,
+    w_down,
+    expert_ids,
+    cotangent,
+):
+    seq_length, model_width = tokens.shape
+    block_len, top_count = expert_ids.shape
+    expert_count = w_router.shape[1]
+    local_experts = w_gate.shape[0]
+    local_heads = w_query.shape[1] // HD
+    quarters = lax.axis_size("tensor")
+    device_count = quarters * lax.axis_size("expert")
+    quarter = lax.axis_index("tensor")
+    device = lax.axis_index(BOTH)
+    first_expert = lax.axis_index("expert") * local_experts
+    pair_cap = 2 * (3 * block_len * top_count // (2 * expert_count))
+    score_scale = HD ** (-0.5)
+    narrow = jnp.bfloat16
+
+    def swap(value, even, odd=None):
+        odd = even if odd is None else odd
+        perm = [(i, i ^ (odd if i & 1 else even)) for i in range(device_count)]
+        return lax.ppermute(value, BOTH, perm)
+
+    def gather_plane(own):
+        first = swap(own, ACROSS, ASIDE)
+        second = swap(own, ASIDE, ACROSS)
+        both = swap(first, ASIDE, ACROSS)
+        mine = [own, first, second, both]
+        return jnp.concatenate(mine + [swap(part, CORE) for part in mine], axis=0)
+
+    def gather_chunks(own):
+        return [gather_plane(own if m == 0 else swap(own, m)) for m in PLANES]
+
+    def reduce_plane(parts):
+        parts = parts.reshape(8, block_len, model_width)
+        mine = parts[:4] + swap(parts[4:], CORE)
+        back = swap(mine[3], ASIDE, ACROSS)
+        side = swap(mine[2], ASIDE, ACROSS)
+        return mine[0] + side + swap(mine[1] + back, ACROSS, ASIDE)
+
+    def reduce_chunks(chunks):
+        sums = [reduce_plane(chunk) for chunk in chunks]
+        total = sums[0].astype(jnp.float32)
+        for mask, part in zip(PLANES[1:], sums[1:]):
+            total = total + swap(part, mask).astype(jnp.float32)
+        return total
+
+    def slot_sources():
+        odd = device & 1
+        sources = []
+        for mask in PLANES:
+            for partner in (0, 1):
+                base = device ^ mask ^ partner
+                flipped = odd ^ partner
+                near = jnp.where(flipped == 0, ACROSS, ASIDE)
+                far = jnp.where(flipped == 0, ASIDE, ACROSS)
+                sources += [base, base ^ near, base ^ far, base ^ near ^ far]
+        return jnp.stack(sources)
+
+    grad_chunks_in = gather_chunks(cotangent)
+    ids_all = lax.all_gather(expert_ids, BOTH, axis=0, tiled=False)
+    sources = slot_sources()
+    ids_by_slot = jnp.take(ids_all, sources, axis=0)
+
+    order = quarter ^ jnp.arange(quarters, dtype=jnp.int32)
+    by_block = tokens.reshape(quarters, block_len, model_width)
+    inputs = jnp.concatenate(
+        [lax.dynamic_slice_in_dim(by_block, order[r], 1, 0)[0] for r in range(quarters)], axis=0
+    ).astype(jnp.float32)
+    positions = (order[:, None] * block_len + jnp.arange(block_len, dtype=jnp.int32)).reshape(-1)
+    inverse_one, normed_one = norm_forward(inputs, gain_attn)
+    hidden_one = normed_one.astype(narrow)
+    frequency = jnp.exp(
+        -jnp.log(theta_base) * jnp.arange(HD // 2, dtype=jnp.float32) * (2.0 / HD)
+    )
+    angles = positions.astype(jnp.float32)[:, None] * frequency[None, :]
+    cosine_table, sine_table = (jnp.cos(angles)[:, None, :], jnp.sin(angles)[:, None, :])
+
+    def project(weights):
+        return jnp.dot(hidden_one, weights, preferred_element_type=jnp.float32).reshape(
+            seq_length, local_heads, HD
+        )
+
+    queries = rotate(project(w_query), cosine_table, sine_table).astype(narrow)
+    key_rows = rotate(project(w_key), cosine_table, sine_table).astype(narrow)
+    value_rows = project(w_value).astype(narrow)
+    allowed = positions[:, None] >= positions[None, :]
+
+    def masked_scores():
+        scores = jnp.einsum("qhd,khd->hqk", queries, key_rows, preferred_element_type=jnp.float32)
+        return jnp.where(allowed, scores * score_scale, masked)
+
+    scores = masked_scores()
+    row_max = jnp.max(scores, axis=-1, keepdims=True)
+    exponent = jnp.exp(scores - row_max)
+    row_total = jnp.sum(exponent, axis=-1, keepdims=True)
+    weights = (exponent / row_total).astype(narrow)
+    head_out = jnp.einsum("hqk,khd->qhd", weights, value_rows, preferred_element_type=jnp.float32)
+    log_total = row_max + jnp.log(row_total)
+    head_rows = head_out.astype(narrow).reshape(seq_length, local_heads * HD)
+
+    def reduce_quarters(full):
+        parts = full.reshape(quarters, block_len, model_width)
+        sent = swap(jnp.stack([parts[1], parts[3]]).astype(narrow), CORE)
+        away = (parts[2] + sent[1].astype(jnp.float32)).astype(narrow)
+        return parts[0] + sent[0].astype(jnp.float32) + swap(away, ACROSS).astype(jnp.float32)
+
+    attention = reduce_quarters(jnp.dot(head_rows, w_out, preferred_element_type=jnp.float32))
+    own_inputs = inputs[:block_len]
+    own_inverse = inverse_one[:block_len]
+    middle = own_inputs + attention
+    inverse_two, normed_two = norm_forward(middle, gain_moe)
+    hidden_two = normed_two.astype(narrow)
+    logits = jnp.dot(hidden_two, w_router, preferred_element_type=jnp.float32)
+    expert_range = jnp.arange(expert_count, dtype=jnp.int32)
+    matches = expert_ids[:, :, None] == expert_range[None, None, :]
+    chosen = jnp.sum(jnp.where(matches, logits[:, None, :], 0.0), axis=2)
+    gate_weights = jax.nn.softmax(chosen, axis=-1)
+
+    row_chunks_in = gather_chunks(hidden_two)
+    local_range = first_expert + jnp.arange(local_experts, dtype=jnp.int32)
+
+    def expert_chunk(rows_in, grads_in, ids):
+        pairs = ids.shape[0] // 2
+        tokens_in = 2 * block_len
+        ids = ids.reshape(pairs, tokens_in, top_count)
+        named = jnp.any(ids[..., None] == expert_range, axis=2)
+        scored = jnp.dot(rows_in, w_router, preferred_element_type=jnp.float32)
+        scored = jnp.where(named, scored.reshape(pairs, tokens_in, expert_count), masked)
+        gates = jax.nn.softmax(scored, axis=-1)
+        gates = lax.dynamic_slice_in_dim(gates, first_expert, local_experts, 2)
+        hits = jnp.any(ids[..., None] == local_range, axis=2)
+        counts = hits.astype(jnp.int32)
+        slot = jnp.where(hits, jnp.cumsum(counts, axis=1) - counts, -1)
+        pick = slot.transpose(0, 2, 1)[:, :, None, :] == jnp.arange(pair_cap)[:, None]
+        select = pick.astype(narrow).reshape(pairs, local_experts * pair_cap, tokens_in)
+        row_gates = jnp.sum(jnp.where(pick, gates.transpose(0, 2, 1)[:, :, None, :], 0.0), axis=3)
+        row_gates = row_gates.transpose(1, 0, 2).reshape(local_experts, pairs * pair_cap, 1)
+
+        def spread(source):
+            source = source.reshape(pairs, tokens_in, model_width)
+            out = jnp.einsum("prt,ptd->prd", select, source, preferred_element_type=narrow)
+            out = out.reshape(pairs, local_experts, pair_cap, model_width)
+            return out.transpose(1, 0, 2, 3).reshape(local_experts, pairs * pair_cap, model_width)
+
+        def combine(rows):
+            rows = rows.astype(narrow).reshape(local_experts, pairs, pair_cap, model_width)
+            rows = rows.transpose(1, 0, 2, 3).reshape(pairs, -1, model_width)
+            out = jnp.einsum("prt,prd->ptd", select, rows, preferred_element_type=jnp.float32)
+            return out.astype(narrow)
+
+        rows = spread(rows_in)
+        row_grads = spread(grads_in)
+        gate_pre = jnp.einsum("lrd,ldf->lrf", rows, w_gate, preferred_element_type=jnp.float32)
+        up_pre = jnp.einsum("lrd,ldf->lrf", rows, w_up, preferred_element_type=jnp.float32)
+        plain = jnp.einsum("lrd,lfd->lrf", row_grads, w_down, preferred_element_type=jnp.float32)
+        sigmoid_gate = jax.nn.sigmoid(gate_pre)
+        silu_gate = gate_pre * sigmoid_gate
+        activation = silu_gate * up_pre
+        gate_sums = jnp.sum(activation * plain, axis=2)
+        grad_act = row_gates * plain
+        gated = (row_gates * activation).astype(narrow)
+        grad_gate = grad_act * up_pre * sigmoid_gate * (1.0 + gate_pre * (1.0 - sigmoid_gate))
+        grad_gate = grad_gate.astype(narrow)
+        grad_up = (grad_act * silu_gate).astype(narrow)
+        forward_rows = jnp.einsum("lrf,lfd->lrd", gated, w_down, preferred_element_type=jnp.float32)
+        back_rows = jnp.einsum("lrf,ldf->lrd", grad_gate, w_gate, preferred_element_type=jnp.float32)
+        back_rows = back_rows + jnp.einsum(
+            "lrf,ldf->lrd", grad_up, w_up, preferred_element_type=jnp.float32
+        )
+        gate_sums = gate_sums.reshape(local_experts, pairs, pair_cap).transpose(1, 0, 2)
+        gate_sums = jnp.sum(jnp.where(pick, gate_sums[..., None], 0.0), axis=2)
+        gate_sums = gate_sums.reshape(pairs, local_experts, 2, block_len).transpose(0, 2, 1, 3)
+        gate_sums = gate_sums.reshape(2 * pairs, local_experts, block_len)
+        kept = (rows, row_grads, gated, grad_gate, grad_up)
+        return (combine(forward_rows), combine(back_rows), gate_sums, kept)
+
+    mixed_parts, back_parts, sums_parts, kept_parts = [], [], [], []
+    for index, (rows_in, grads_in) in enumerate(zip(row_chunks_in, grad_chunks_in)):
+        done = expert_chunk(rows_in, grads_in, ids_by_slot[8 * index : 8 * index + 8])
+        mixed_parts.append(done[0])
+        back_parts.append(done[1])
+        sums_parts.append(done[2])
+        kept_parts.append(done[3])
+
+    slot_sums = jnp.concatenate(sums_parts, axis=0)
+    place = jnp.sum(
+        jnp.where(sources[None, :] == jnp.arange(device_count)[:, None], jnp.arange(device_count), 0),
+        axis=1,
+    )
+    wide = jnp.zeros((device_count, expert_count, block_len), jnp.float32)
+    wide = lax.dynamic_update_slice_in_dim(
+        wide, jnp.take(slot_sums, place, axis=0), first_expert, 1
+    )
+    own_sums = lax.psum_scatter(wide, BOTH, scatter_dimension=0, tiled=True)[0].T
+
+    grad_out = cotangent.astype(jnp.float32)
+    grad_hidden_disp = reduce_chunks(back_parts)
+    grad_gates = jnp.sum(jnp.where(matches, own_sums[:, None, :], 0.0), axis=2)
+    grad_chosen = gate_weights * (
+        grad_gates - jnp.sum(gate_weights * grad_gates, axis=-1, keepdims=True)
+    )
+    grad_logits = jnp.sum(jnp.where(matches, grad_chosen[:, :, None], 0.0), axis=1).astype(narrow)
+    grad_router = jnp.einsum(
+        "ld,le->de", hidden_two, grad_logits, preferred_element_type=jnp.float32
+    )
+    grad_hidden_two = grad_hidden_disp + jnp.einsum(
+        "le,de->ld", grad_logits, w_router, preferred_element_type=jnp.float32
+    )
+    grad_normed_two, grad_gain_moe = norm_backward(middle, inverse_two, gain_moe, grad_hidden_two)
+    grad_middle = grad_out + grad_normed_two
+    grad_attn = grad_middle.astype(narrow)
+
+    across = swap(grad_attn, ACROSS)
+    grad_attn_all = jnp.concatenate(
+        [grad_attn, swap(grad_attn, CORE), across, swap(across, CORE)], axis=0
+    )
+    mixed_parts, grad_attn_all = lax.optimization_barrier((mixed_parts, grad_attn_all))
+    mixed_out = (middle + reduce_chunks(mixed_parts)).astype(narrow)
+
+    kept = [jnp.concatenate(parts, axis=1) for parts in zip(*kept_parts)]
+    rows_all, row_grads_all, gated_all, grad_gate_all, grad_up_all = kept
+    grad_w_down = jnp.einsum(
+        "lrf,lrd->lfd", gated_all, row_grads_all, preferred_element_type=jnp.float32
+    )
+    grad_w_gate = jnp.einsum(
+        "lrd,lrf->ldf", rows_all, grad_gate_all, preferred_element_type=jnp.float32
+    )
+    grad_w_up = jnp.einsum("lrd,lrf->ldf", rows_all, grad_up_all, preferred_element_type=jnp.float32)
+
+    grad_w_out = jnp.einsum(
+        "lh,ld->hd", head_rows, grad_attn_all, preferred_element_type=jnp.float32
+    )
+    grad_heads = (
+        jnp.einsum("ld,hd->lh", grad_attn_all, w_out, preferred_element_type=jnp.float32)
+        .astype(narrow)
+        .reshape(seq_length, local_heads, HD)
+    )
+    probability = jnp.exp(masked_scores() - log_total)
+    grad_values = jnp.einsum(
+        "hqk,qhd->khd", probability.astype(narrow), grad_heads, preferred_element_type=jnp.float32
+    )
+    grad_prob = jnp.einsum(
+        "qhd,khd->hqk", grad_heads, value_rows, preferred_element_type=jnp.float32
+    )
+    row_delta = jnp.sum(probability * grad_prob, axis=-1, keepdims=True)
+    grad_scores = (probability * (grad_prob - row_delta)).astype(narrow)
+    grad_query = score_scale * jnp.einsum(
+        "hqk,khd->qhd", grad_scores, key_rows, preferred_element_type=jnp.float32
+    )
+    grad_keys = score_scale * jnp.einsum(
+        "hqk,qhd->khd", grad_scores, queries, preferred_element_type=jnp.float32
+    )
+
+    def flat(source):
+        return source.astype(narrow).reshape(seq_length, local_heads * HD)
+
+    grad_query_raw = flat(rotate(grad_query, cosine_table, -sine_table))
+    grad_key_raw = flat(rotate(grad_keys, cosine_table, -sine_table))
+    grad_value_raw = flat(grad_values)
+
+    def weight_grad(grad_raw):
+        return jnp.einsum("ld,lh->dh", hidden_one, grad_raw, preferred_element_type=jnp.float32)
+
+    def back(grad_raw, weights):
+        return jnp.einsum("lh,dh->ld", grad_raw, weights, preferred_element_type=jnp.float32)
+
+    grad_hidden_one = reduce_quarters(
+        back(grad_query_raw, w_query) + back(grad_key_raw, w_key) + back(grad_value_raw, w_value)
+    )
+    grad_normed_one, grad_gain_attn = norm_backward(
+        own_inputs, own_inverse, gain_attn, grad_hidden_one
+    )
+    grad_tokens = grad_middle + grad_normed_one
+    attn_sums = lax.psum(
+        tuple(
+            part.astype(narrow)
+            for part in (
+                weight_grad(grad_query_raw),
+                weight_grad(grad_key_raw),
+                weight_grad(grad_value_raw),
+                grad_w_out,
+            )
+        ),
+        "expert",
+    )
+    attn_sums = [part.astype(jnp.float32) for part in attn_sums]
+    small = jnp.concatenate([grad_router, grad_gain_attn[:, None], grad_gain_moe[:, None]], axis=1)
+    small = lax.psum(small, BOTH)
+    return (
+        mixed_out,
+        grad_tokens,
+        small[:, expert_count],
+        attn_sums[0],
+        attn_sums[1],
+        attn_sums[2],
+        attn_sums[3],
+        small[:, expert_count + 1],
+        small[:, :expert_count],
+        grad_w_gate,
+        grad_w_up,
+        grad_w_down,
+    )
+
+
+def on_device(*operands):
+    tokens, w_router, w_gate, expert_ids = operands[0], operands[7], operands[8], operands[11]
+    owners, quarters = lax.axis_size("expert"), lax.axis_size("tensor")
+    block_len, top_count = expert_ids.shape
+    capacity = 3 * block_len * top_count // (2 * w_router.shape[1])
+    buffer_rows = capacity * quarters * owners * w_gate.shape[0]
+    gathers = owners * tokens.shape[0] <= buffer_rows and (owners, quarters) == (8, 4)
+    return (gathered_layer if gathers else routed_layer)(*operands)
 
 
 def solution(mesh):

time: 2240 us -> 1480 us (0.66)
  waiting for transfers between devices: 1340 us -> 599 us
  blocking collectives: 324 us -> 40.2 us
  matrix products: 240 us -> 377 us
  starting transfers between devices: 11.3 us -> 67.4 us
  other arithmetic: 81.8 us -> 117 us
    unnamed x9 -> x3, waiting for transfers between devices: 343 us -> 0.05 us
    all_to_all x2 -> x0, blocking collectives: 285 us -> none  [the longest x1 144 us: on_device(): lax.all_to_all(send_rows, 'expert', split_axis=1, concat_axis=1, tiled=True)]
    psum x2, waiting for transfers between devices: 583 us -> 310 us  [the longest x1 272 us: gathered_layer(): lax.psum(tuple((part.astype(narrow) for part in (weight_grad(grad_query_r...]
    all_to_all x2 -> x0, waiting for transfers between devices: 234 us -> none  [the longest x1 125 us: on_device(): lax.all_to_all(row_grads.reshape(capacity, expert_count, model_width), 'e...]
    ppermute x0 -> x107, waiting for transfers between devices: none -> 187 us  [swap(): return lax.ppermute(value, BOTH, perm)]
    dot_general x31 -> x68, matrix products: 240 us -> 377 us  [the longest x4 50.6 us: expert_chunk(): jnp.einsum('lrf,ldf->lrd', grad_up, w_up, preferred_element_type=jnp.floa...]
    all_gather x3 -> x0, waiting for transfers between devices: 132 us -> none  [the longest x1 131 us: on_device(): lax.all_gather(grads_in, 'tensor', axis=0, tiled=True)]
    ppermute x0 -> x107, starting transfers between devices: none -> 66.9 us  [swap(): return lax.ppermute(value, BOTH, perm)]
  transfers between devices with their start and end apart: 10 -> 110, of which waited for: 8 -> 32; matrix products, arithmetic and copies ran while one was open for 8% -> 46% of each run, Pallas kernels for 0% -> 0%
where the time goes in v1:
time: 1480 us; the launch traced here: 1470 us
  waiting for transfers between devices  599 us (40%)
  matrix products  377 us (25%)
  local copies, waits for them, and re-layouts  241 us (16%)
  other arithmetic  117 us (8%)
  starting transfers between devices  67.4 us (5%)
  blocking collectives  40.2 us (3%)
  between operations  24.4 us (2%)
    psum x1, waiting for transfers between devices, gathered_layer(): lax.psum(tuple((part.astype(narrow) for part in (weight_grad(grad_query_r...  272 us
    ppermute x107, waiting for transfers between devices, swap(): return lax.ppermute(value, BOTH, perm)  187 us
    reduce_scatter x1, waiting for transfers between devices, gathered_layer(): lax.psum_scatter(wide, BOTH, scatter_dimension=0, tiled=True)[0]  102 us
    unnamed x391, local copies, waits for them, and re-layouts  94 us
    ppermute x107, starting transfers between devices, swap(): return lax.ppermute(value, BOTH, perm)  66.9 us
    dot_general x4, matrix products, expert_chunk(): jnp.einsum('lrf,ldf->lrd', grad_up, w_up, preferred_element_type=jnp.floa...  50.6 us
    reshape x4, local copies, waits for them, and re-layouts, spread(): out.transpose(1, 0, 2, 3)  43.8 us
    all_gather x1, blocking collectives, gathered_layer(): ids_all = lax.all_gather(expert_ids, BOTH, axis=0, tiled=False)  40.2 us
  transfers between devices with their start and end apart: 110, of which 32 were waited for; matrix products, arithmetic and copies ran while one was open for 46% of the time, Pallas kernels for 0%

profile of v1, /device:TPU:0, one launch (start us, length us, event | category | flops | bytes accessed | tf_op | source)
XLA Modules:
  0.0 1465.9 jit_solution(1602675998915290384)
XLA Ops:
  65.2 40.2 %all-gather = s32[4096,8]{0,1:T(8,128)S(1)} all-gather(s32[128,8]{0,1:T(8,128)S(1)} %copy-done.134), channel_id=2, replica_groups=mesh['expert'=8,'tensor'=4] {'expert','tensor'}, dimensions={0}, use_global_device_ids=true | all-gather | bytes 135168 | tf_op jit(solution)/shard_map/all_gather | solution.py:416
  177.3 13.1 collective-permute-done.1
  341.9 11.6 fusion.166
  353.5 12.7 add_convert_fusion.3
  382.9 11.2 copy.441
  493.5 10.8 copy.444
  504.3 10.8 copy.443
  515.2 10.8 copy.442
  526.8 10.3 multiply_reduce_fusion.2
  539.6 10.3 multiply_reduce_fusion.3
  552.4 10.3 multiply_reduce_fusion.4
  568.9 11.8 fusion.168
  580.7 12.6 add_convert_fusion.2
  612.1 12.8 add_convert_fusion.1
  643.7 12.6 add_convert_fusion
  664.8 17.4 %fusion = f32[8,256,2048]{2,1,0:T(8,128)} fusion(bf16[8,192,2048]{2,1,0:T(8,128)(2,1)} %bitcast.652, bf16[8,192,2048]{2,1,0:T(8,128)(2,1)} %bitcast.654, bf16[8,192,2048]{2,1,0:T(8,128)(2,1)} %bitcast.656, bf16[8,192,2048]{2,1,0:T(8,128)(2,1)} %bitcast.650, bf16[8,192,256]{2,1,0:T(8,128)(2,1)} %get-tuple-element.78, ...), kind=kOutput, calls=%fused_computation.3 | convolution fusion | flops 6555697152 | bytes 45088768 | tf_op jit(solution)/shard_map/lrf,lrd->lfd/dot_general | solution.py:578
  682.2 22.7 %fusion.18 = f32[8,2048,256]{2,1,0:T(8,128)} fusion(bf16[8,192,256]{2,1,0:T(8,128)(2,1)} %copy-done.75, bf16[8,192,256]{2,1,0:T(8,128)(2,1)} %copy-done.74, bf16[8,192,256]{2,1,0:T(8,128)(2,1)} %copy-done.73, bf16[8,192,256]{2,1,0:T(8,128)(2,1)} %get-tuple-element.67, bf16[8,192,2048]{1,2,0:T(8,128)(2,1)} %copy.444, bf16[8,192,2048]{1,2,0:T(8,128)(2,1)} %copy.443, ...), kind=kOutput, calls=%fused_computation.46 | convolution fusion | flops 6555697152 | bytes 45088768 | tf_op jit(solution)/shard_map/lrd,lrf->ldf/dot_general | solution.py:584
  756.1 102.1 %reduce-scatter.2.cloned.1.call-done = f32[1,64,128]{2,1,0:T(8,128)} async-done(((f32[32,64,128]{2,1,0:T(8,128)}), f32[1,64,128]{2,1,0:T(8,128)}) %reduce-scatter.2.cloned.1.call-update) | async-done | bytes 32784 | tf_op jit(solution)/shard_map/reduce_scatter | solution.py:550
  864.8 20.6 %collective-permute-done.80 = bf16[128,2048]{1,0:T(8,128)(2,1)S(1)} collective-permute-done((bf16[128,2048]{1,0:T(8,128)(2,1)S(1)}, bf16[128,2048]{1,0:T(8,128)(2,1)S(1)}, u32[]{:S(2)}, u32[]{:S(2)}) %collective-permute-start.80) | collective-permute-done | bytes 524320 | tf_op jit(solution)/shard_map/ppermute | solution.py:377
  906.1 22.6 %collective-permute-done.69 = bf16[128,2048]{1,0:T(8,128)(2,1)S(1)} collective-permute-done((bf16[128,2048]{1,0:T(8,128)(2,1)S(1)}, bf16[128,2048]{1,0:T(8,128)(2,1)S(1)}, u32[]{:S(2)}, u32[]{:S(2)}) %collective-permute-start.69) | collective-permute-done | bytes 524320 | tf_op jit(solution)/shard_map/ppermute | solution.py:377
  1025.5 22.7 %fusion.10 = f32[8,2048,256]{2,1,0:T(8,128)} fusion(bf16[8,192,256]{2,1,0:T(8,128)(2,1)} %copy-done.79, bf16[8,192,256]{2,1,0:T(8,128)(2,1)} %copy-done.78, bf16[8,192,256]{2,1,0:T(8,128)(2,1)} %copy-done.77, bf16[8,192,256]{2,1,0:T(8,128)(2,1)} %copy-done.76, bf16[8,192,2048]{1,2,0:T(8,128)(2,1)} %copy.444, bf16[8,192,2048]{1,2,0:T(8,128)(2,1)} %copy.443, ...), kind=kOutput, calls=%fused_computation.38 | convolution fusion | flops 6555697152 | bytes 45088768 | tf_op jit(solution)/shard_map/lrd,lrf->ldf/dot_general | solution.py:581
  1085.3 16.7 %collective-permute-done.102 = bf16[128,2048]{1,0:T(8,128)(2,1)S(1)} collective-permute-done((bf16[128,2048]{1,0:T(8,128)(2,1)S(1)}, bf16[128,2048]{1,0:T(8,128)(2,1)S(1)}, u32[]{:S(2)}, u32[]{:S(2)}) %collective-permute-start.102) | collective-permute-done | bytes 524320 | tf_op jit(solution)/shard_map/ppermute | solution.py:377
  1130.3 38.5 %all-reduce.4.cloned.1.call-done = f32[2048,66]{0,1:T(8,128)} async-done(((f32[2048,66]{0,1:T(8,128)}), f32[2048,66]{0,1:T(8,128)}) %all-reduce.4.cloned.1.call-update) | async-done | bytes 540688 | tf_op jit(solution)/shard_map/psum | solution.py:644
  1175.4 271.7 %all-reduce.6.cloned.1.call-done = (bf16[2048,512]{1,0:T(8,128)(2,1)}, bf16[2048,512]{1,0:T(8,128)(2,1)}, bf16[2048,512]{1,0:T(8,128)(2,1)}, bf16[512,2048]{1,0:T(8,128)(2,1)}) async-done(((bf16[2048,512]{1,0:T(8,128)(2,1)}, bf16[2048,512]{1,0:T(8,128)(2,1)}, bf16[2048,512]{1,0:T(8,128)(2,1)}, bf16[512,2048]{1,0:T(8,128)(2,1)}), (bf16[2048,512]{1,0:T(8,128)(2,1)}, bf16[2048,512]{1,0:T(8,128)(2,1)}, ...) | async-done | bytes 8388624 | tf_op jit(solution)/shard_map/psum | solution.py:630
  (906 shorter events, 704.5 us)
Async XLA Ops:
  7.2 850.9 %reduce-scatter.2.cloned.1.call-start = ((), (), s32[]{:S(2)}) async-start(), calls=%async_computation.1 | async-start | bytes 1081344 | tf_op jit(solution)/shard_map/reduce_scatter | solution.py:550
  7.2 120.8 %collective-permute-start.70 = (bf16[128,2048]{1,0:T(8,128)(2,1)}, bf16[128,2048]{1,0:T(8,128)(2,1)}, u32[]{:S(2)}, u32[]{:S(2)}) collective-permute-start(bf16[128,2048]{1,0:T(8,128)(2,1)} %param.25), channel_id=1, source_target_pairs={{0,24},{1,25},{2,26},{3,27},{4,28},{5,29},{6,30},{7,31},{8,16},{9,... | collective-permute-start | bytes 1572872 | tf_op jit(solution)/shard_map/ppermute | solution.py:377
  12.4 118.0 %collective-permute-start.57 = (bf16[128,2048]{1,0:T(8,128)(2,1)}, bf16[128,2048]{1,0:T(8,128)(2,1)}, u32[]{:S(2)}, u32[]{:S(2)}) collective-permute-start(bf16[128,2048]{1,0:T(8,128)(2,1)} %param.25), channel_id=1, source_target_pairs={{0,16},{1,17},{2,18},{3,19},{4,20},{5,21},{6,22},{7,23},{8,24},{9,... | collective-permute-start | bytes 1572872 | tf_op jit(solution)/shard_map/ppermute | solution.py:377
  12.4 120.2 %collective-permute-start.44 = (bf16[128,2048]{1,0:T(8,128)(2,1)}, bf16[128,2048]{1,0:T(8,128)(2,1)}, u32[]{:S(2)}, u32[]{:S(2)}) collective-permute-start(bf16[128,2048]{1,0:T(8,128)(2,1)} %param.25), channel_id=1, source_target_pairs={{0,8},{1,9},{2,10},{3,11},{4,12},{5,13},{6,14},{7,15},{8,0},{9,1},... | collective-permute-start | bytes 1572872 | tf_op jit(solution)/shard_map/ppermute | solution.py:377
  13.0 121.5 %collective-permute-start.33 = (bf16[128,2048]{1,0:T(8,128)(2,1)}, bf16[128,2048]{1,0:T(8,128)(2,1)}, u32[]{:S(2)}, u32[]{:S(2)}) collective-permute-start(bf16[128,2048]{1,0:T(8,128)(2,1)} %param.25), channel_id=1, source_target_pairs={{0,2},{1,5},{2,0},{3,7},{4,6},{5,1},{6,4},{7,3},{8,10},{9,13},{10,... | collective-permute-start | bytes 1572872 | tf_op jit(solution)/shard_map/ppermute | solution.py:377
  14.6 120.9 %collective-permute-start.34 = (bf16[128,2048]{1,0:T(8,128)(2,1)}, bf16[128,2048]{1,0:T(8,128)(2,1)}, u32[]{:S(2)}, u32[]{:S(2)}) collective-permute-start(bf16[128,2048]{1,0:T(8,128)(2,1)} %param.25), channel_id=1, source_target_pairs={{0,4},{1,3},{2,6},{3,1},{4,0},{5,7},{6,2},{7,5},{8,12},{9,11},{10,... | collective-permute-start | bytes 1572872 | tf_op jit(solution)/shard_map/ppermute | solution.py:377
  135.6 62.7 %collective-permute-start.74 = (bf16[128,2048]{1,0:T(8,128)(2,1)}, bf16[128,2048]{1,0:T(8,128)(2,1)S(1)}, u32[]{:S(2)}, u32[]{:S(2)}) collective-permute-start(bf16[128,2048]{1,0:T(8,128)(2,1)} %collective-permute-done.70), channel_id=1, source_target_pairs={{0,1},{1,0},{2,3},{3,2},{4,5},{5,4},{6,7},{7,6},{8,9},{9,8},{10,11... | collective-permute-start | bytes 1572872 | tf_op jit(solution)/shard_map/ppermute | solution.py:377
  258.8 109.5 %collective-permute-start.29 = (bf16[128,2048]{1,0:T(8,128)(2,1)}, bf16[128,2048]{1,0:T(8,128)(2,1)}, u32[]{:S(2)}, u32[]{:S(2)}) collective-permute-start(bf16[128,2048]{1,0:T(8,128)(2,1)} %collective-permute-done.25), channel_id=1, source_target_pairs={{0,1},{1,0},{2,3},{3,2},{4,5},{5,4},{6,7},{7,6},{8,9},{9,8},{10,11... | collective-permute-start | bytes 1572872 | tf_op jit(solution)/shard_map/ppermute | solution.py:377
  289.9 91.2 %collective-permute-start.21 = (bf16[128,2048]{1,0:T(8,128)(2,1)}, bf16[128,2048]{1,0:T(8,128)(2,1)}, u32[]{:S(2)}, u32[]{:S(2)}) collective-permute-start(bf16[128,2048]{1,0:T(8,128)(2,1)} %collective-permute-done.17), channel_id=1, source_target_pairs={{0,1},{1,0},{2,3},{3,2},{4,5},{5,4},{6,7},{7,6},{8,9},{9,8},{10,11... | collective-permute-start | bytes 1572872 | tf_op jit(solution)/shard_map/ppermute | solution.py:377
  300.6 109.2 %collective-permute-start.13 = (bf16[128,2048]{1,0:T(8,128)(2,1)}, bf16[128,2048]{1,0:T(8,128)(2,1)}, u32[]{:S(2)}, u32[]{:S(2)}) collective-permute-start(bf16[128,2048]{1,0:T(8,128)(2,1)} %collective-permute-done.9), channel_id=1, source_target_pairs={{0,1},{1,0},{2,3},{3,2},{4,5},{5,4},{6,7},{7,6},{8,9},{9,8},{10,11... | collective-permute-start | bytes 1572872 | tf_op jit(solution)/shard_map/ppermute | solution.py:377
  300.8 65.4 %collective-permute-start.28 = (bf16[128,2048]{1,0:T(8,128)(2,1)}, bf16[128,2048]{1,0:T(8,128)(2,1)}, u32[]{:S(2)}, u32[]{:S(2)}) collective-permute-start(bf16[128,2048]{1,0:T(8,128)(2,1)} %collective-permute-done.26), channel_id=1, source_target_pairs={{0,4},{1,3},{2,6},{3,1},{4,0},{5,7},{6,2},{7,5},{8,12},{9,11},{10,... | collective-permute-start | bytes 1572872 | tf_op jit(solution)/shard_map/ppermute | solution.py:377
  301.6 70.0 %collective-permute-start.30 = (bf16[128,2048]{1,0:T(8,128)(2,1)}, bf16[128,2048]{1,0:T(8,128)(2,1)}, u32[]{:S(2)}, u32[]{:S(2)}) collective-permute-start(bf16[128,2048]{1,0:T(8,128)(2,1)} %collective-permute-done.26), channel_id=1, source_target_pairs={{0,1},{1,0},{2,3},{3,2},{4,5},{5,4},{6,7},{7,6},{8,9},{9,8},{10,11... | collective-permute-start | bytes 1572872 | tf_op jit(solution)/shard_map/ppermute | solution.py:377
  405.0 326.3 %collective-permute-start.40 = (bf16[4,128,2048]{2,1,0:T(8,128)(2,1)}, bf16[4,128,2048]{2,1,0:T(8,128)(2,1)}, u32[]{:S(2)}, u32[]{:S(2)}) collective-permute-start(bf16[4,128,2048]{2,1,0:T(8,128)(2,1)} %bitcast.157), channel_id=1, source_target_pairs={{0,1},{1,0},{2,3},{3,2},{4,5},{5,4},{6,7},{7,6},{8,9},{9,8},{10,11... | collective-permute-start | bytes 6291464 | tf_op jit(solution)/shard_map/ppermute | solution.py:377
  601.6 144.1 %collective-permute-start.52 = (bf16[4,128,2048]{2,1,0:T(8,128)(2,1)}, bf16[4,128,2048]{2,1,0:T(8,128)(2,1)}, u32[]{:S(2)}, u32[]{:S(2)}) collective-permute-start(bf16[4,128,2048]{2,1,0:T(8,128)(2,1)} %bitcast.170), channel_id=1, source_target_pairs={{0,1},{1,0},{2,3},{3,2},{4,5},{5,4},{6,7},{7,6},{8,9},{9,8},{10,11... | collective-permute-start | bytes 6291464 | tf_op jit(solution)/shard_map/ppermute | solution.py:377
  633.3 118.1 %collective-permute-start.65 = (bf16[4,128,2048]{2,1,0:T(8,128)(2,1)}, bf16[4,128,2048]{2,1,0:T(8,128)(2,1)}, u32[]{:S(2)}, u32[]{:S(2)}) collective-permute-start(bf16[4,128,2048]{2,1,0:T(8,128)(2,1)} %bitcast.183), channel_id=1, source_target_pairs={{0,1},{1,0},{2,3},{3,2},{4,5},{5,4},{6,7},{7,6},{8,9},{9,8},{10,11... | collective-permute-start | bytes 6291464 | tf_op jit(solution)/shard_map/ppermute | solution.py:377
  664.4 194.6 %collective-permute-start.78 = (bf16[4,128,2048]{2,1,0:T(8,128)(2,1)}, bf16[4,128,2048]{2,1,0:T(8,128)(2,1)}, u32[]{:S(2)}, u32[]{:S(2)}) collective-permute-start(bf16[4,128,2048]{2,1,0:T(8,128)(2,1)} %bitcast.196), channel_id=1, source_target_pairs={{0,1},{1,0},{2,3},{3,2},{4,5},{5,4},{6,7},{7,6},{8,9},{9,8},{10,11... | collective-permute-start | bytes 6291464 | tf_op jit(solution)/shard_map/ppermute | solution.py:377
  724.3 444.4 %all-reduce.4.cloned.1.call-start = ((), (), s32[]{:S(2)}) async-start(), calls=%async_computation.2 | async-start | bytes 1179648 | tf_op jit(solution)/shard_map/psum | solution.py:644
  743.4 157.6 %collective-permute-start.41 = (bf16[128,2048]{1,0:T(8,128)(2,1)}, bf16[128,2048]{1,0:T(8,128)(2,1)}, u32[]{:S(2)}, u32[]{:S(2)}) collective-permute-start(bf16[128,2048]{1,0:T(8,128)(2,1)} %get-tuple-element.93), channel_id=1, source_target_pairs={{0,4},{1,3},{2,6},{3,1},{4,0},{5,7},{6,2},{7,5},{8,12},{9,11},{10,... | collective-permute-start | bytes 1572872 | tf_op jit(solution)/shard_map/ppermute | solution.py:377
  749.3 113.1 %collective-permute-start.54 = (bf16[128,2048]{1,0:T(8,128)(2,1)}, bf16[128,2048]{1,0:T(8,128)(2,1)S(1)}, u32[]{:S(2)}, u32[]{:S(2)}) collective-permute-start(bf16[128,2048]{1,0:T(8,128)(2,1)} %get-tuple-element.96), channel_id=1, source_target_pairs={{0,4},{1,3},{2,6},{3,1},{4,0},{5,7},{6,2},{7,5},{8,12},{9,11},{10,... | collective-permute-start | bytes 1572872 | tf_op jit(solution)/shard_map/ppermute | solution.py:377
  749.9 135.5 %collective-permute-start.53 = (bf16[128,2048]{1,0:T(8,128)(2,1)}, bf16[128,2048]{1,0:T(8,128)(2,1)}, u32[]{:S(2)}, u32[]{:S(2)}) collective-permute-start(bf16[128,2048]{1,0:T(8,128)(2,1)} %get-tuple-element.95), channel_id=1, source_target_pairs={{0,4},{1,3},{2,6},{3,1},{4,0},{5,7},{6,2},{7,5},{8,12},{9,11},{10,... | collective-permute-start | bytes 1572872 | tf_op jit(solution)/shard_map/ppermute | solution.py:377
  755.4 109.2 %collective-permute-start.67 = (bf16[128,2048]{1,0:T(8,128)(2,1)}, bf16[128,2048]{1,0:T(8,128)(2,1)S(1)}, u32[]{:S(2)}, u32[]{:S(2)}) collective-permute-start(bf16[128,2048]{1,0:T(8,128)(2,1)} %get-tuple-element.98), channel_id=1, source_target_pairs={{0,4},{1,3},{2,6},{3,1},{4,0},{5,7},{6,2},{7,5},{8,12},{9,11},{10,... | collective-permute-start | bytes 1572872 | tf_op jit(solution)/shard_map/ppermute | solution.py:377
  1020.9 426.2 %all-reduce.6.cloned.1.call-start = ((), (), s32[]{:S(2)}) async-start(), calls=%async_computation.3 | async-start | bytes 16777216 | tf_op jit(solution)/shard_map/psum | solution.py:630
  1053.9 118.3 %collective-permute-start.87 = (bf16[128,2048]{1,0:T(8,128)(2,1)}, bf16[128,2048]{1,0:T(8,128)(2,1)}, u32[]{:S(2)}, u32[]{:S(2)}) collective-permute-start(bf16[128,2048]{1,0:T(8,128)(2,1)} %get-tuple-element.85), channel_id=1, source_target_pairs={{0,4},{1,3},{2,6},{3,1},{4,0},{5,7},{6,2},{7,5},{8,12},{9,11},{10,... | collective-permute-start | bytes 1572872 | tf_op jit(solution)/shard_map/ppermute | solution.py:377
  1106.3 65.8 %collective-permute-start.89 = (bf16[128,2048]{1,0:T(8,128)(2,1)}, bf16[128,2048]{1,0:T(8,128)(2,1)}, u32[]{:S(2)}, u32[]{:S(2)}) collective-permute-start(bf16[128,2048]{1,0:T(8,128)(2,1)} %fusion.65), channel_id=1, source_target_pairs={{0,2},{1,5},{2,0},{3,7},{4,6},{5,1},{6,4},{7,3},{8,10},{9,13},{10,... | collective-permute-start | bytes 1572872 | tf_op jit(solution)/shard_map/ppermute | solution.py:377
  (252 other events, 4313.3 us)
Sparse Core Ops, SparseCore 0:
  724.5 133.6 reduce-scatter.1
  1021.0 147.7 all-reduce.3
  1173.3 273.6 all-reduce.5
